TPU v7x, 128 devices: a whole 4x4x4 slice. The times are simulated.
128 devices in a mesh: row: 8 (over z, y_hi), col: 16 (over x, y_lo, core).
Axes of the slice: x: 4, y: 4 (y_hi: 2, y_lo: 2; y = y_hi * 2 + y_lo), z: 4, core: 2. Of those that a mesh axis runs over, the one named last changes fastest.
Arguments:
- obj: float32 [2, 2048, 4096], P(None, 'row', 'col'), may hold values from -4.2 to 4.2
- probe: float32 [2, 256, 256], replicated, may hold values from -4.2 to 4.2
- amplitudes: bfloat16 [512, 256, 256], P(('row', 'col')), may hold values from 0.049804688 to 4
- positions: int32 [512, 2], replicated, may hold values from 0 to 3840, as said below
Outputs:
- new_object: float32 [2, 2048, 4096], P(None, 'row', 'col')
- new_probe: float32 [2, 256, 256], replicated
Inputs may be any that keep to these rules, and one draw needn't show every extreme that they name: `positions`: entry p is the top-left cell (row, column) of pattern p's window of 256 x 256 cells, which lies inside the object. Pattern p is held by device p // 4 in row-major order of (row, col), and its row offset lies in that device's band of 256 object rows. One device holds at most 2 patterns whose window starts in one tile, and exactly 2 for some tile in every draw; at most 8 windows start in one tile, and in every row of tiles exactly 8 start in one tile.
All inputs are finite; a program needn't handle non-finite values.
Results may differ from a plain program's by a relative error of at most 0.0018.
Values may be sent and summed in bfloat16 or wider, within the bound.
A program may use at most 128 MiB of HBM per device.

v0:
```python
import jax
import jax.numpy as jnp
from jax import lax
from jax.sharding import PartitionSpec as P

ITERS = 2
SEND = 2
amplitude_floor = 0.1
object_regular = 0.5
probe_regular = 1.0
highest = lax.Precision.HIGHEST


def passed_along(value, axis, steps):
    count = lax.axis_size(axis)
    leading, last = (max(0, -steps), min(count, count - steps))
    return lax.ppermute(value, axis, [(source, source + steps) for source in range(leading, last)])


def dft_tables(order):
    counter = jnp.arange(order, dtype=jnp.int32)
    phases = counter[:, None] * counter[None, :] % order
    angles = phases.astype(jnp.float32) * (2.0 * jnp.pi / order)
    norming = 1.0 / jnp.sqrt(jnp.float32(order))
    return (jnp.cos(angles) * norming, -jnp.sin(angles) * norming)


def left_apply(tables, real_part, imag_part):
    first = jnp.einsum("ab,sbc->sac", tables[0], real_part, precision=highest)
    second = jnp.einsum("ab,sbc->sac", tables[1], imag_part, precision=highest)
    third = jnp.einsum("ab,sbc->sac", tables[2], real_part + imag_part, precision=highest)
    return (first - second, third - first - second)


def right_apply(tables, real_part, imag_part):
    first = jnp.einsum("sab,bc->sac", real_part, tables[0], precision=highest)
    second = jnp.einsum("sab,bc->sac", imag_part, tables[1], precision=highest)
    third = jnp.einsum("sab,bc->sac", real_part + imag_part, tables[2], precision=highest)
    return (first - second, third - first - second)


def transform(tables, real_part, imag_part):
    inner_re, inner_im = right_apply(tables, real_part, imag_part)
    return left_apply(tables, inner_re, inner_im)


def extend_tile(current):
    from_right = passed_along(current, "col", -1)
    widened = jnp.concatenate([current, from_right], axis=2)
    from_below = passed_along(widened, "row", -1)
    return jnp.concatenate([widened, from_below], axis=1)


def fold_tile(sums, tile_rows, tile_cols, order):
    from_above = passed_along(sums[:, tile_rows:, :], "row", 1)
    upper = sums[:, :tile_rows, :].at[:, :order, :].add(from_above)
    from_left = passed_along(upper[:, :, tile_cols:], "col", 1)
    return upper[:, :, :tile_cols].at[:, :, :order].add(from_left)


def local(obj, probe, amplitudes, positions):
    col_count = lax.axis_size("col")
    my_row = lax.axis_index("row")
    my_col = lax.axis_index("col")
    device_id = my_row * col_count + my_col
    tile_rows = obj.shape[1]
    tile_cols = obj.shape[2]
    order = probe.shape[1]
    pat_count = amplitudes.shape[0]
    capacity = 2 * pat_count
    slot_count = col_count * SEND
    band_count = col_count * pat_count
    local_index = jnp.arange(pat_count, dtype=jnp.int32)
    my_ids = device_id * pat_count + local_index
    owner_col = positions[my_ids, 1] // tile_cols
    earlier = local_index[None, :] < local_index[:, None]
    same_owner = owner_col[:, None] == owner_col[None, :]
    send_rank = jnp.sum(same_owner & earlier, axis=1)
    send_slot = owner_col * SEND + send_rank
    placing = (jnp.arange(slot_count, dtype=jnp.int32)[:, None] == send_slot[None, :]).astype(
        jnp.bfloat16
    )
    outgoing = jnp.dot(
        placing, amplitudes.reshape(pat_count, order * order), preferred_element_type=jnp.float32
    ).astype(jnp.bfloat16)
    incoming = lax.all_to_all(outgoing, "col", split_axis=0, concat_axis=0, tiled=True)
    band_first = my_row * band_count
    band_pos = lax.dynamic_slice_in_dim(positions, band_first, band_count, 0)
    band_ids = band_first + jnp.arange(band_count, dtype=jnp.int32)
    in_mine = band_pos[:, 1] // tile_cols == my_col
    mine_count = in_mine.astype(jnp.int32)
    band_rank = jnp.cumsum(mine_count) - mine_count
    selection = (band_rank[None, :] == jnp.arange(capacity, dtype=jnp.int32)[:, None]) & in_mine[
        None, :
    ]
    valid = jnp.any(selection, axis=1)
    listed = jnp.sum(jnp.where(selection, band_ids[None, :], 0), axis=1)
    source_dev = listed // pat_count
    source_col = source_dev % col_count
    before = (
        (source_dev[None, :] == source_dev[:, None])
        & (listed[None, :] < listed[:, None])
        & valid[None, :]
    )
    recv_rank = jnp.sum(before, axis=1)
    recv_slot = source_col * SEND + recv_rank
    picking = (
        (jnp.arange(slot_count, dtype=jnp.int32)[None, :] == recv_slot[:, None]) & valid[:, None]
    ).astype(jnp.bfloat16)
    measured = jnp.dot(picking, incoming, preferred_element_type=jnp.float32).reshape(
        capacity, order, order
    )
    spots = positions[listed]
    offset_y = jnp.where(valid, spots[:, 0] - my_row * tile_rows, 0)
    offset_x = jnp.where(valid, spots[:, 1] - my_col * tile_cols, 0)
    weight = valid.astype(jnp.float32)[:, None, None]
    cos_part, sin_part = dft_tables(order)
    forward = (cos_part, sin_part, cos_part + sin_part)
    inverse = (cos_part, -sin_part, cos_part - sin_part)
    current = obj
    probe_now = probe
    for sweep in range(ITERS):
        extended = extend_tile(current)

        def cut_window(top, left):
            return lax.dynamic_slice(extended, (0, top, left), (2, order, order))

        windows = jax.vmap(cut_window)(offset_y, offset_x)
        win_re = windows[:, 0]
        win_im = windows[:, 1]
        probe_re = probe_now[0]
        probe_im = probe_now[1]
        exit_re = probe_re * win_re - probe_im * win_im
        exit_im = probe_re * win_im + probe_im * win_re
        far_re, far_im = transform(forward, exit_re, exit_im)
        factor = measured / jnp.sqrt(far_re * far_re + far_im * far_im + amplitude_floor)
        back_re, back_im = transform(inverse, far_re * factor, far_im * factor)
        change_re = (back_re - exit_re) * weight
        change_im = (back_im - exit_im) * weight
        power = probe_re * probe_re + probe_im * probe_im
        deposits = jnp.stack(
            [
                probe_re * change_re + probe_im * change_im,
                probe_re * change_im - probe_im * change_re,
                power[None] * weight + 0.0 * change_re,
            ],
            axis=1,
        )

        def deposit(index, total):
            start = (0, offset_y[index], offset_x[index])
            block = lax.dynamic_slice(total, start, (3, order, order))
            return lax.dynamic_update_slice(total, block + deposits[index], start)

        sums = lax.fori_loop(
            0, capacity, deposit, jnp.zeros((3, tile_rows + order, tile_cols + order), jnp.float32)
        )
        partials = jnp.stack(
            [
                jnp.sum(win_re * change_re + win_im * change_im, axis=0),
                jnp.sum(win_re * change_im - win_im * change_re, axis=0),
                jnp.sum((win_re * win_re + win_im * win_im) * weight, axis=0),
            ]
        )
        tile_sums = fold_tile(sums, tile_rows, tile_cols, order)
        current = current + tile_sums[:2] / (tile_sums[2] + object_regular)[None]
        totals = lax.psum(partials, ("row", "col"))
        probe_now = probe_now + totals[:2] / (totals[2] + probe_regular)[None]
    return (current, probe_now)


def solution(mesh):
    placed = (P(None, "row", "col"), P(), P(("row", "col"), None, None), P())
    return jax.shard_map(
        local, mesh=mesh, in_specs=placed, out_specs=(P(None, "row", "col"), P()), check_vma=False
    )
```

profile of v0, /device:TPU:1, one launch (start us, length us, event | category | flops | bytes accessed | tf_op | source)
XLA Modules:
  0.0 974.0 jit_solution(13523694036995378047)
XLA Ops:
  16.7 5.9 all_to_all.8
  22.6 5.7 all-to-all-start
  34.0 65.7 %collective-permute-done.1 = f32[2,256,512]{2,1,0:T(8,128)} collective-permute-done((f32[2,256,512]{2,1,0:T(8,128)S(1)}, f32[2,256,512]{2,1,0:T(8,128)}, u32[]{:S(2)}, u32[]{:S(2)}) %collective-permute-start.1) | collective-permute-done | bytes 1048608 | tf_op jit(solution)/shard_map/ppermute | solution.py:17
  103.5 25.5 %while.38 = (s32[]{:T(128)}, f32[2,512,512]{2,1,0:T(8,128)S(1)}, s32[8,3]{0,1:T(4,128)S(1)}, f32[8,2,256,256]{2,3,0,1:T(8,128)}, s32[]{:T(128)}) while((s32[]{:T(128)}, f32[2,512,512]{2,1,0:T(8,128)S(1)}, s32[8,3]{0,1:T(4,128)S(1)}, f32[8,2,256,256]{2,3,0,1:T(8,128)}, s32[]{:T(128)}) %tuple.156), condition=%wide.while_cond.4, body=%wide.while_body.4.sunk | while | flops 2 | bytes 3145853 | solution.py:126
  140.7 5.0 subtract_subtract_fusion.3
  145.7 5.6 fusion.112
  151.3 5.7 fusion.79
  157.0 5.5 all_to_all.10
  169.6 12.4 %fusion.48 = (f32[8,256,256]{1,2,0:T(8,128)S(1)}, f32[8,256,256]{1,2,0:T(8,128)S(1)}) fusion(f32[8,256,256]{1,2,0:T(8,128)} %copy.167, f32[8,256,256]{2,1,0:T(8,128)} %fusion.112, f32[8,256,256]{2,1,0:T(8,128)} %fusion.79, f32[8,256,256]{2,1,0:T(8,128)} %copy-done.9, f32[8,256,256]{2,1,0:T(8,128)} %copy-done.4, f32[8,256,256]{2,1,0:T(8,128)} %copy-done.3), kind=kOutput, calls=%fused_computation.104 | convolution fusion | flops 1618083840 | bytes 16777216 | tf_op jit(solution)/shard_map/ab,sbc->sac/dot_general | solution.py:31
  190.9 4.9 subtract_subtract_fusion.2
  195.8 4.5 fusion.76
  204.8 6.5 fusion.27
  217.5 134.4 %while.36 = (s32[]{:T(128)}, f32[3,512,512]{2,1,0:T(8,128)}, s32[8]{0:T(128)S(1)}, s32[8]{0:T(128)S(1)}, f32[8,3,256,256]{2,3,0,1:T(8,128)}, /*index=5*/s32[]{:T(128)}, s32[]{:T(128)}, s32[]{:T(128)}) while((s32[]{:T(128)}, f32[3,512,512]{2,1,0:T(8,128)}, s32[8]{0:T(128)S(1)}, s32[8]{0:T(128)S(1)}, f32[8,3,256,256]{2,3,0,1:T(8,128)}, ...), condition=%wide.region_6.7_spmd, body=%wide.region_5.6_spmd.sunk | while | flops 196616 | bytes 7078089 | solution.py:155
  225.6 8.9 dynamic_update_slice.16
  242.7 8.9 dynamic_update_slice.16
  259.7 9.4 dynamic_update_slice.16
  277.2 9.0 dynamic_update_slice.16
  294.3 8.3 dynamic_update_slice.16
  310.7 8.3 dynamic_update_slice.16
  327.2 8.3 dynamic_update_slice.16
  343.6 8.3 dynamic_update_slice.16
  357.5 31.8 %collective-permute-done.2 = f32[3,256,512]{2,1,0:T(8,128)S(1)} collective-permute-done((f32[3,256,512]{2,1,0:T(8,128)S(1)}, f32[3,256,512]{2,1,0:T(8,128)S(1)}, u32[]{:S(2)}, u32[]{:S(2)}) %collective-permute-start.2) | collective-permute-done | bytes 1572896 | tf_op jit(solution)/shard_map/ppermute | solution.py:17
  389.7 6.2 collective-permute-start.3
  396.0 8.9 collective-permute-done.3
  408.2 8.3 collective-permute-done.4
  418.1 147.8 %all-reduce.4.cloned.1.call-done = f32[3,256,256]{1,2,0:T(8,128)} async-done(((f32[3,256,256]{1,2,0:T(8,128)}), f32[3,256,256]{1,2,0:T(8,128)}) %all-reduce.4.cloned.1.call-update) | async-done | bytes 786448 | tf_op jit(solution)/shard_map/psum | solution.py:167
  572.9 25.8 %while.39 = (s32[]{:T(128)}, f32[2,512,512]{2,1,0:T(8,128)S(1)}, s32[8,3]{0,1:T(4,128)S(1)}, f32[8,2,256,256]{2,3,0,1:T(8,128)}, s32[]{:T(128)}) while((s32[]{:T(128)}, f32[2,512,512]{2,1,0:T(8,128)S(1)}, s32[8,3]{0,1:T(4,128)S(1)}, f32[8,2,256,256]{2,3,0,1:T(8,128)}, s32[]{:T(128)}) %tuple.172), condition=%wide.while_cond.5, body=%wide.while_body.5.sunk | while | flops 2 | bytes 3145853 | solution.py:126
  610.5 4.9 subtract_subtract_fusion.1
  615.4 4.5 fusion.73
  624.3 5.5 fusion.38
  634.4 4.6 fusion.117
  639.0 4.6 subtract_subtract_fusion
  643.6 4.5 fusion.70
  648.2 4.7 fusion.96
  652.9 6.9 fusion.12
  666.0 133.6 %while.37 = (s32[]{:T(128)}, f32[3,512,512]{2,1,0:T(8,128)}, s32[8]{0:T(128)S(1)}, s32[8]{0:T(128)S(1)}, f32[8,3,256,256]{2,3,0,1:T(8,128)}, /*index=5*/s32[]{:T(128)}, s32[]{:T(128)}, s32[]{:T(128)}) while((s32[]{:T(128)}, f32[3,512,512]{2,1,0:T(8,128)}, s32[8]{0:T(128)S(1)}, s32[8]{0:T(128)S(1)}, f32[8,3,256,256]{2,3,0,1:T(8,128)}, ...), condition=%wide.region_12.13_spmd, body=%wide.region_11.12_spmd.sunk | while | flops 196616 | bytes 7078089 | solution.py:155
  674.0 8.9 dynamic_update_slice.17
  690.9 8.9 dynamic_update_slice.17
  707.9 9.4 dynamic_update_slice.17
  725.3 9.0 dynamic_update_slice.17
  742.3 8.3 dynamic_update_slice.17
  758.6 8.3 dynamic_update_slice.17
  775.0 8.3 dynamic_update_slice.17
  791.3 8.3 dynamic_update_slice.17
  802.5 5.0 collective-permute-start.6
  808.5 30.1 %collective-permute-done.6 = f32[3,256,512]{2,1,0:T(8,128)} collective-permute-done((f32[3,256,512]{2,1,0:T(8,128)}, f32[3,256,512]{2,1,0:T(8,128)}, u32[]{:S(2)}, u32[]{:S(2)}) %collective-permute-start.6) | collective-permute-done | bytes 1572896 | tf_op jit(solution)/shard_map/ppermute | solution.py:17
  841.6 5.9 collective-permute-start.7
  847.6 114.0 %all-reduce.6.cloned.1.call-done = f32[3,256,256]{1,2,0:T(8,128)} async-done(((f32[3,256,256]{1,2,0:T(8,128)}), f32[3,256,256]{1,2,0:T(8,128)}) %all-reduce.6.cloned.1.call-update) | async-done | bytes 786448 | tf_op jit(solution)/shard_map/psum | solution.py:167
  (314 shorter events, 232.4 us)
Async XLA Ops:
  7.2 23.1 %collective-permute-start = (f32[2,256,256]{2,1,0:T(8,128)}, f32[2,256,256]{2,1,0:T(8,128)S(1)}, u32[]{:S(2)}, u32[]{:S(2)}) collective-permute-start(f32[2,256,256]{2,1,0:T(8,128)} %param.24), channel_id=1, source_target_pairs={{1,0},{2,1},{3,2},{4,3},{5,4},{6,5},{7,6},{8,7},{9,8},{10,9},{11,1... | collective-permute-start | bytes 1572872 | tf_op jit(solution)/shard_map/ppermute | solution.py:17
  22.6 5.7 copy-start
  22.6 7.4 copy-start.19
  22.6 134.4 %all-to-all-start = ((bf16[16,2,65536]{2,1,0:T(2,128)(2,1)}), bf16[16,2,65536]{2,1,0:T(2,128)(2,1)}, u32[]{:S(2)}, u32[]{:S(2)}) async-start(bf16[16,2,65536]{2,1,0:T(2,128)(2,1)} %all_to_all.8), calls=%async_computation | async-start | bytes 8388608 | tf_op jit(solution)/shard_map/all_to_all | solution.py:86
  28.3 3.6 copy-start.21
  28.3 537.6 %all-reduce.4.cloned.1.call-start = ((), (), s32[]{:S(2)}) async-start(), calls=%async_computation.1 | async-start | bytes 1572864 | tf_op jit(solution)/shard_map/psum | solution.py:167
  30.4 69.3 %collective-permute-start.1 = (f32[2,256,512]{2,1,0:T(8,128)S(1)}, f32[2,256,512]{2,1,0:T(8,128)}, u32[]{:S(2)}, u32[]{:S(2)}) collective-permute-start(f32[2,256,512]{2,1,0:T(8,128)S(1)} %constant_dynamic-update-slice_fusion.2), channel_id=1, source_target_pairs={{16,0},{32,16},{48,32},{64,48},{80,64},{96,80},{112,96},{17,1},{33... | collective-permute-start | bytes 3145736 | tf_op jit(solution)/shard_map/ppermute | solution.py:17
  131.8 8.9 copy-start.1
  136.2 15.1 %copy-start.3 = (f32[8,256,256]{2,1,0:T(8,128)}, f32[8,256,256]{2,1,0:T(8,128)S(1)}, u32[]{:S(2)}) copy-start(f32[8,256,256]{2,1,0:T(8,128)S(1)} %fusion.114) | copy-start | bytes 6291460
  140.7 10.6 %copy-start.4 = (f32[8,256,256]{2,1,0:T(8,128)}, f32[8,256,256]{2,1,0:T(8,128)S(1)}, u32[]{:S(2)}) copy-start(f32[8,256,256]{2,1,0:T(8,128)S(1)} %fusion.126) | copy-start | bytes 6291460
  145.7 5.6 copy-start.9
  195.8 9.0 copy-start.7
  200.3 4.5 copy-start.2
  204.8 6.5 copy-start.18
  204.8 6.5 copy-start.29
  352.0 37.3 %copy-start.6 = (f32[3,512,512]{2,1,0:T(8,128)S(1)}, f32[3,512,512]{2,1,0:T(8,128)}, u32[]{:S(2)}) copy-start(f32[3,512,512]{2,1,0:T(8,128)} %get-tuple-element.270) | copy-start | bytes 9437188
  353.7 35.6 %collective-permute-start.2 = (f32[3,256,512]{2,1,0:T(8,128)S(1)}, f32[3,256,512]{2,1,0:T(8,128)S(1)}, u32[]{:S(2)}, u32[]{:S(2)}) collective-permute-start(f32[3,256,512]{2,1,0:T(8,128)S(1)} %slice.165), channel_id=1, source_target_pairs={{0,16},{16,32},{32,48},{48,64},{64,80},{80,96},{96,112},{1,17},{17... | collective-permute-start | bytes 4718600 | tf_op jit(solution)/shard_map/ppermute | solution.py:17
  389.6 15.4 %copy-start.20 = (f32[2,256,256]{2,1,0:T(8,128)S(1)}, f32[2,256,256]{2,1,0:T(8,128)}, u32[]{:S(2)}) copy-start(f32[2,256,256]{2,1,0:T(8,128)} %param.24) | copy-start | bytes 1572868
  389.7 15.2 %collective-permute-start.3 = (f32[3,256,256]{2,1,0:T(8,128)S(1)}, f32[3,256,256]{2,1,0:T(8,128)S(1)}, u32[]{:S(2)}, u32[]{:S(2)}) collective-permute-start(f32[3,256,256]{2,1,0:T(8,128)S(1)} %slice.219), channel_id=1, source_target_pairs={{0,1},{1,2},{2,3},{3,4},{4,5},{5,6},{6,7},{7,8},{8,9},{9,10},{10,1... | collective-permute-start | bytes 2359304 | tf_op jit(solution)/shard_map/ppermute | solution.py:17
  405.2 163.9 %copy-start.11 = (f32[2,256,256]{2,1,0:T(8,128)}, f32[2,256,256]{2,1,0:T(8,128)S(1)}, u32[]{:S(2)}) copy-start(f32[2,256,256]{2,1,0:T(8,128)S(1)} %fusion.84) | copy-start | bytes 1572868
  405.2 11.2 %collective-permute-start.4 = (f32[2,256,256]{2,1,0:T(8,128)S(1)}, f32[2,256,256]{2,1,0:T(8,128)S(1)}, u32[]{:S(2)}, u32[]{:S(2)}) collective-permute-start(f32[2,256,256]{2,1,0:T(8,128)S(1)} %fusion.84), channel_id=1, source_target_pairs={{1,0},{2,1},{3,2},{4,3},{5,4},{6,5},{7,6},{8,7},{9,8},{10,9},{11,1... | collective-permute-start | bytes 1572872 | tf_op jit(solution)/shard_map/ppermute | solution.py:17
  407.1 10.8 %copy-start.22 = (f32[2,256,256]{2,1,0:T(8,128)S(1)}, f32[2,256,256]{2,1,0:T(8,128)}, u32[]{:S(2)}) copy-start(f32[2,256,256]{2,1,0:T(8,128)} %param.25) | copy-start | bytes 1572868
  408.1 553.5 %all-reduce.6.cloned.1.call-start = ((), (), s32[]{:S(2)}) async-start(), calls=%async_computation.2 | async-start | bytes 1572864 | tf_op jit(solution)/shard_map/psum | solution.py:167
  416.4 1.4 copy-start.23
  416.6 152.5 %collective-permute-start.5 = (f32[2,256,512]{2,1,0:T(8,128)S(1)}, f32[2,256,512]{2,1,0:T(8,128)}, u32[]{:S(2)}, u32[]{:S(2)}) collective-permute-start(f32[2,256,512]{2,1,0:T(8,128)S(1)} %pad_maximum_fusion.4), channel_id=1, source_target_pairs={{16,0},{32,16},{48,32},{64,48},{80,64},{96,80},{112,96},{17,1},{33... | collective-permute-start | bytes 3145736 | tf_op jit(solution)/shard_map/ppermute | solution.py:17
  565.9 3.2 copy-start.24
  568.1 1.0 copy-start.15
  619.9 4.5 copy-start.10
  648.1 4.7 copy-start.8
  652.8 6.9 copy-start.17
  652.8 6.9 copy-start.28
  799.7 7.9 copy-start.25
  799.7 7.9 copy-start.26
  799.7 7.9 copy-start.27
  799.7 38.9 %copy-start.5 = (f32[3,512,512]{2,1,0:T(8,128)S(1)}, f32[3,512,512]{2,1,0:T(8,128)}, u32[]{:S(2)}) copy-start(f32[3,512,512]{2,1,0:T(8,128)} %get-tuple-element.271) | copy-start | bytes 9437188
  802.5 36.1 %collective-permute-start.6 = (f32[3,256,512]{2,1,0:T(8,128)}, f32[3,256,512]{2,1,0:T(8,128)}, u32[]{:S(2)}, u32[]{:S(2)}) collective-permute-start(f32[3,256,512]{2,1,0:T(8,128)} %slice.177), channel_id=1, source_target_pairs={{0,16},{16,32},{32,48},{48,64},{64,80},{80,96},{96,112},{1,17},{17... | collective-permute-start | bytes 4718600 | tf_op jit(solution)/shard_map/ppermute | solution.py:17
  840.4 1.2 copy-start.13
  841.5 121.0 %copy-start.16 = (f32[2,256,256]{1,2,0:T(8,128)S(1)}, f32[2,256,256]{1,2,0:T(8,128)}, u32[]{:S(2)}) copy-start(f32[2,256,256]{1,2,0:T(8,128)} %copy-done.15) | copy-start | bytes 1572868
  841.6 123.1 %copy-start.14 = (f32[3,256,512]{2,1,0:T(8,128)S(1)}, f32[3,256,512]{2,1,0:T(8,128)}, u32[]{:S(2)}) copy-start(f32[3,256,512]{2,1,0:T(8,128)} %copy-done.13) | copy-start | bytes 4718596
  841.6 123.1 %collective-permute-start.7 = (f32[3,256,256]{2,1,0:T(8,128)S(1)}, f32[3,256,256]{2,1,0:T(8,128)}, u32[]{:S(2)}, u32[]{:S(2)}) collective-permute-start(f32[3,256,256]{2,1,0:T(8,128)S(1)} %slice.227), channel_id=1, source_target_pairs={{0,1},{1,2},{2,3},{3,4},{4,5},{5,6},{6,7},{7,8},{8,9},{9,10},{10,1... | collective-permute-start | bytes 2359304 | tf_op jit(solution)/shard_map/ppermute | solution.py:17
  963.7 2.3 copy-start.12
Sparse Core Ops, SparseCore 0:
  408.2 157.6 all-reduce.3
  808.6 152.9 all-reduce.5
where the time goes:
time: 985 us; the launch traced here: 974 us
  waiting for transfers between devices  407 us (41%)
  local copies, waits for them, and re-layouts  268 us (27%)
  matrix products  132 us (13%)
  loops' own time  61.9 us (6%)
  other arithmetic  55.1 us (6%)
  starting transfers between devices  34.6 us (4%)
  between operations  15.1 us (2%)
    psum x2, waiting for transfers between devices, local(): totals = lax.psum(partials, ('row', 'col'))  262 us
    ppermute x8, waiting for transfers between devices, passed_along(): lax.ppermute(value, axis, [(source, source + steps) for source in range(l...  145 us
    dynamic_update_slice x16, local copies, waits for them, and re-layouts, deposit(): return lax.dynamic_update_slice(total, block + deposits[index], start)  139 us
    another operation x2, loops' own time, local(): lax.fori_loop(0, capacity, deposit, jnp.zeros((3, tile_rows + order, tile...  61.4 us
    gather x80, local copies, waits for them, and re-layouts  50.8 us
    dot_general x4, matrix products, left_apply(): jnp.einsum('ab,sbc->sac', tables[2], real_part + imag_part, precision=hig...  31.3 us
    ppermute x8, starting transfers between devices, passed_along(): lax.ppermute(value, axis, [(source, source + steps) for source in range(l...  28.9 us
    add x16, other arithmetic, deposit(): return lax.dynamic_update_slice(total, block + deposits[index], start)  25.4 us
  transfers between devices with their start and end apart: 11, of which 7 were waited for; matrix products, arithmetic and copies ran while one was open for 8% of the time, Pallas kernels for 0%

commit v1 on v0

--- a/solution.py
+++ b/solution.py
@@ -164,7 +164,9 @@
         )
         tile_sums = fold_tile(sums, tile_rows, tile_cols, order)
         current = current + tile_sums[:2] / (tile_sums[2] + object_regular)[None]
-        totals = lax.psum(partials, ("row", "col"))
+        totals = partials
+        for name in ("row", "col"):
+            totals = lax.psum(totals, name)
         probe_now = probe_now + totals[:2] / (totals[2] + probe_regular)[None]
     return (current, probe_now)
 

time: 985 us -> 1090 us (1.11)
  waiting for transfers between devices: 407 us -> 505 us
    psum x2 -> x4, waiting for transfers between devices: 262 us -> 399 us  [local(): totals = lax.psum(totals, name)]
    ppermute x8, waiting for transfers between devices: 145 us -> 106 us  [passed_along(): lax.ppermute(value, axis, [(source, source + steps) for source in range(l...]
  transfers between devices with their start and end apart: 11 -> 13, of which waited for: 7 -> 7; matrix products, arithmetic and copies ran while one was open for 8% -> 7% of each run, Pallas kernels for 0% -> 0%
where the time goes in v1:
time: 1090 us; the launch traced here: 1080 us
  waiting for transfers between devices  505 us (46%)
  local copies, waits for them, and re-layouts  269 us (25%)
  matrix products  132 us (12%)
  loops' own time  61.9 us (6%)
  other arithmetic  56.2 us (5%)
  starting transfers between devices  37.7 us (3%)
  between operations  14.8 us (1%)
    psum x4, waiting for transfers between devices, local(): totals = lax.psum(totals, name)  399 us
    dynamic_update_slice x16, local copies, waits for them, and re-layouts, deposit(): return lax.dynamic_update_slice(total, block + deposits[index], start)  139 us
    ppermute x8, waiting for transfers between devices, passed_along(): lax.ppermute(value, axis, [(source, source + steps) for source in range(l...  106 us
    another operation x2, loops' own time, local(): lax.fori_loop(0, capacity, deposit, jnp.zeros((3, tile_rows + order, tile...  61.4 us
    gather x80, local copies, waits for them, and re-layouts  50.8 us
    ppermute x8, starting transfers between devices, passed_along(): lax.ppermute(value, axis, [(source, source + steps) for source in range(l...  31.9 us
    dot_general x4, matrix products, left_apply(): jnp.einsum('ab,sbc->sac', tables[2], real_part + imag_part, precision=hig...  31.3 us
    add x16, other arithmetic, deposit(): return lax.dynamic_update_slice(total, block + deposits[index], start)  25.4 us
  transfers between devices with their start and end apart: 13, of which 7 were waited for; matrix products, arithmetic and copies ran while one was open for 7% of the time, Pallas kernels for 0%

profile of v1, /device:TPU:1, one launch (start us, length us, event | category | flops | bytes accessed | tf_op | source)
XLA Modules:
  0.0 1076.8 jit_solution(1513861480384165769)
XLA Ops:
  16.7 5.9 all_to_all.8
  22.6 5.7 all-to-all-start
  34.0 65.7 %collective-permute-done.1 = f32[2,256,512]{2,1,0:T(8,128)} collective-permute-done((f32[2,256,512]{2,1,0:T(8,128)S(1)}, f32[2,256,512]{2,1,0:T(8,128)}, u32[]{:S(2)}, u32[]{:S(2)}) %collective-permute-start.1) | collective-permute-done | bytes 1048608 | tf_op jit(solution)/shard_map/ppermute | solution.py:17
  103.5 25.5 %while.38 = (s32[]{:T(128)}, f32[2,512,512]{2,1,0:T(8,128)S(1)}, s32[8,3]{0,1:T(4,128)S(1)}, f32[8,2,256,256]{2,3,0,1:T(8,128)}, s32[]{:T(128)}) while((s32[]{:T(128)}, f32[2,512,512]{2,1,0:T(8,128)S(1)}, s32[8,3]{0,1:T(4,128)S(1)}, f32[8,2,256,256]{2,3,0,1:T(8,128)}, s32[]{:T(128)}) %tuple.156), condition=%wide.while_cond.4, body=%wide.while_body.4.sunk | while | flops 2 | bytes 3145853 | solution.py:126
  140.7 5.0 subtract_subtract_fusion.3
  145.7 5.6 fusion.112
  151.3 5.7 fusion.79
  157.0 5.5 all_to_all.10
  169.6 12.4 %fusion.48 = (f32[8,256,256]{1,2,0:T(8,128)S(1)}, f32[8,256,256]{1,2,0:T(8,128)S(1)}) fusion(f32[8,256,256]{1,2,0:T(8,128)} %copy.167, f32[8,256,256]{2,1,0:T(8,128)} %fusion.112, f32[8,256,256]{2,1,0:T(8,128)} %fusion.79, f32[8,256,256]{2,1,0:T(8,128)} %copy-done.9, f32[8,256,256]{2,1,0:T(8,128)} %copy-done.4, f32[8,256,256]{2,1,0:T(8,128)} %copy-done.3), kind=kOutput, calls=%fused_computation.104 | convolution fusion | flops 1618083840 | bytes 16777216 | tf_op jit(solution)/shard_map/ab,sbc->sac/dot_general | solution.py:31
  190.9 4.9 subtract_subtract_fusion.2
  195.8 4.5 fusion.76
  204.8 6.5 fusion.27
  217.5 134.4 %while.36 = (s32[]{:T(128)}, f32[3,512,512]{2,1,0:T(8,128)}, s32[8]{0:T(128)S(1)}, s32[8]{0:T(128)S(1)}, f32[8,3,256,256]{2,3,0,1:T(8,128)}, /*index=5*/s32[]{:T(128)}, s32[]{:T(128)}, s32[]{:T(128)}) while((s32[]{:T(128)}, f32[3,512,512]{2,1,0:T(8,128)}, s32[8]{0:T(128)S(1)}, s32[8]{0:T(128)S(1)}, f32[8,3,256,256]{2,3,0,1:T(8,128)}, ...), condition=%wide.region_6.7_spmd, body=%wide.region_5.6_spmd.sunk | while | flops 196616 | bytes 7078089 | solution.py:155
  225.6 8.9 dynamic_update_slice.16
  242.7 8.9 dynamic_update_slice.16
  259.7 9.4 dynamic_update_slice.16
  277.2 9.0 dynamic_update_slice.16
  294.3 8.3 dynamic_update_slice.16
  310.7 8.3 dynamic_update_slice.16
  327.2 8.3 dynamic_update_slice.16
  343.6 8.3 dynamic_update_slice.16
  357.5 31.8 %collective-permute-done.2 = f32[3,256,512]{2,1,0:T(8,128)S(1)} collective-permute-done((f32[3,256,512]{2,1,0:T(8,128)S(1)}, f32[3,256,512]{2,1,0:T(8,128)S(1)}, u32[]{:S(2)}, u32[]{:S(2)}) %collective-permute-start.2) | collective-permute-done | bytes 1572896 | tf_op jit(solution)/shard_map/ppermute | solution.py:17
  390.6 6.1 collective-permute-start.3
  397.7 8.2 collective-permute-done.3
  409.5 77.4 %all-reduce.6.cloned.1.call-done = f32[3,256,256]{1,2,0:T(8,128)} async-done(((f32[3,256,256]{1,2,0:T(8,128)}), f32[3,256,256]{1,2,0:T(8,128)}) %all-reduce.6.cloned.1.call-update) | async-done | bytes 786448 | tf_op jit(solution)/shard_map/psum | solution.py:169
  488.6 123.1 %all-reduce.8.cloned.1.call-done = f32[3,256,256]{1,2,0:T(8,128)} async-done(((f32[3,256,256]{1,2,0:T(8,128)}), f32[3,256,256]{1,2,0:T(8,128)}) %all-reduce.8.cloned.1.call-update) | async-done | bytes 786448 | tf_op jit(solution)/shard_map/psum | solution.py:169
  618.6 25.8 %while.39 = (s32[]{:T(128)}, f32[2,512,512]{2,1,0:T(8,128)S(1)}, s32[8,3]{0,1:T(4,128)S(1)}, f32[8,2,256,256]{2,3,0,1:T(8,128)}, s32[]{:T(128)}) while((s32[]{:T(128)}, f32[2,512,512]{2,1,0:T(8,128)S(1)}, s32[8,3]{0,1:T(4,128)S(1)}, f32[8,2,256,256]{2,3,0,1:T(8,128)}, s32[]{:T(128)}) %tuple.176), condition=%wide.while_cond.5, body=%wide.while_body.5.sunk | while | flops 2 | bytes 3145853 | solution.py:126
  656.2 4.9 subtract_subtract_fusion.1
  661.1 4.5 fusion.73
  670.1 5.5 fusion.38
  680.1 4.6 fusion.117
  684.7 4.6 subtract_subtract_fusion
  689.4 4.5 fusion.70
  693.9 4.7 fusion.96
  698.6 6.9 fusion.12
  711.8 133.6 %while.37 = (s32[]{:T(128)}, f32[3,512,512]{2,1,0:T(8,128)}, s32[8]{0:T(128)S(1)}, s32[8]{0:T(128)S(1)}, f32[8,3,256,256]{2,3,0,1:T(8,128)}, /*index=5*/s32[]{:T(128)}, s32[]{:T(128)}, s32[]{:T(128)}) while((s32[]{:T(128)}, f32[3,512,512]{2,1,0:T(8,128)}, s32[8]{0:T(128)S(1)}, s32[8]{0:T(128)S(1)}, f32[8,3,256,256]{2,3,0,1:T(8,128)}, ...), condition=%wide.region_13.14_spmd, body=%wide.region_12.13_spmd.sunk | while | flops 196616 | bytes 7078089 | solution.py:155
  719.8 8.9 dynamic_update_slice.17
  736.7 8.9 dynamic_update_slice.17
  753.6 9.4 dynamic_update_slice.17
  771.0 9.0 dynamic_update_slice.17
  788.0 8.3 dynamic_update_slice.17
  804.4 8.3 dynamic_update_slice.17
  820.7 8.3 dynamic_update_slice.17
  837.1 8.3 dynamic_update_slice.17
  848.2 6.0 collective-permute-start.6
  855.2 85.7 %all-reduce.10.cloned.1.call-done = f32[3,256,256]{1,2,0:T(8,128)} async-done(((f32[3,256,256]{1,2,0:T(8,128)}), f32[3,256,256]{1,2,0:T(8,128)}) %all-reduce.10.cloned.1.call-update) | async-done | bytes 786448 | tf_op jit(solution)/shard_map/psum | solution.py:169
  943.9 8.0 collective-permute-start.7
  951.9 112.8 %all-reduce.12.cloned.1.call-done = f32[3,256,256]{1,2,0:T(8,128)} async-done(((f32[3,256,256]{1,2,0:T(8,128)}), f32[3,256,256]{1,2,0:T(8,128)}) %all-reduce.12.cloned.1.call-update) | async-done | bytes 786448 | tf_op jit(solution)/shard_map/psum | solution.py:169
  (320 shorter events, 234.6 us)
Async XLA Ops:
  7.2 23.1 %collective-permute-start = (f32[2,256,256]{2,1,0:T(8,128)}, f32[2,256,256]{2,1,0:T(8,128)S(1)}, u32[]{:S(2)}, u32[]{:S(2)}) collective-permute-start(f32[2,256,256]{2,1,0:T(8,128)} %param.24), channel_id=1, source_target_pairs={{1,0},{2,1},{3,2},{4,3},{5,4},{6,5},{7,6},{8,7},{9,8},{10,9},{11,1... | collective-permute-start | bytes 1572872 | tf_op jit(solution)/shard_map/ppermute | solution.py:17
  22.6 5.7 copy-start
  22.6 7.4 copy-start.19
  22.6 134.4 %all-to-all-start = ((bf16[16,2,65536]{2,1,0:T(2,128)(2,1)}), bf16[16,2,65536]{2,1,0:T(2,128)(2,1)}, u32[]{:S(2)}, u32[]{:S(2)}) async-start(bf16[16,2,65536]{2,1,0:T(2,128)(2,1)} %all_to_all.8), calls=%async_computation | async-start | bytes 8388608 | tf_op jit(solution)/shard_map/all_to_all | solution.py:86
  28.3 3.6 copy-start.21
  28.3 458.5 %all-reduce.6.cloned.1.call-start = ((), (), s32[]{:S(2)}) async-start(), calls=%async_computation.1 | async-start | bytes 1572864 | tf_op jit(solution)/shard_map/psum | solution.py:169
  30.4 69.3 %collective-permute-start.1 = (f32[2,256,512]{2,1,0:T(8,128)S(1)}, f32[2,256,512]{2,1,0:T(8,128)}, u32[]{:S(2)}, u32[]{:S(2)}) collective-permute-start(f32[2,256,512]{2,1,0:T(8,128)S(1)} %constant_dynamic-update-slice_fusion.2), channel_id=1, source_target_pairs={{16,0},{32,16},{48,32},{64,48},{80,64},{96,80},{112,96},{17,1},{33... | collective-permute-start | bytes 3145736 | tf_op jit(solution)/shard_map/ppermute | solution.py:17
  131.8 8.9 copy-start.1
  136.2 15.1 %copy-start.3 = (f32[8,256,256]{2,1,0:T(8,128)}, f32[8,256,256]{2,1,0:T(8,128)S(1)}, u32[]{:S(2)}) copy-start(f32[8,256,256]{2,1,0:T(8,128)S(1)} %fusion.114) | copy-start | bytes 6291460
  140.7 10.6 copy-start.4
  145.7 5.6 copy-start.9
  195.8 9.0 copy-start.7
  200.3 4.5 copy-start.2
  204.8 6.5 copy-start.18
  204.8 6.5 copy-start.29
  352.0 37.3 %copy-start.6 = (f32[3,512,512]{2,1,0:T(8,128)S(1)}, f32[3,512,512]{2,1,0:T(8,128)}, u32[]{:S(2)}) copy-start(f32[3,512,512]{2,1,0:T(8,128)} %get-tuple-element.270) | copy-start | bytes 9437188
  353.7 35.6 %collective-permute-start.2 = (f32[3,256,512]{2,1,0:T(8,128)S(1)}, f32[3,256,512]{2,1,0:T(8,128)S(1)}, u32[]{:S(2)}, u32[]{:S(2)}) collective-permute-start(f32[3,256,512]{2,1,0:T(8,128)S(1)} %slice.165), channel_id=1, source_target_pairs={{0,16},{16,32},{32,48},{48,64},{64,80},{80,96},{96,112},{1,17},{17... | collective-permute-start | bytes 4718600 | tf_op jit(solution)/shard_map/ppermute | solution.py:17
  390.6 15.3 %collective-permute-start.3 = (f32[3,256,256]{2,1,0:T(8,128)}, f32[3,256,256]{2,1,0:T(8,128)}, u32[]{:S(2)}, u32[]{:S(2)}) collective-permute-start(f32[3,256,256]{2,1,0:T(8,128)} %slice.219), channel_id=1, source_target_pairs={{0,1},{1,2},{2,3},{3,4},{4,5},{5,6},{6,7},{7,8},{8,9},{9,10},{10,1... | collective-permute-start | bytes 2359304 | tf_op jit(solution)/shard_map/ppermute | solution.py:17
  397.7 9.6 copy-start.20
  397.7 214.0 %all-reduce.8.cloned.1.call-start = ((), (), s32[]{:S(2)}) async-start(), calls=%async_computation.2 | async-start | bytes 1572864 | tf_op jit(solution)/shard_map/psum | solution.py:169
  407.3 81.1 %copy-start.22 = (f32[2,256,256]{2,1,0:T(8,128)S(1)}, f32[2,256,256]{2,1,0:T(8,128)}, u32[]{:S(2)}) copy-start(f32[2,256,256]{2,1,0:T(8,128)} %param.25) | copy-start | bytes 1572868
  407.4 207.4 %copy-start.11 = (f32[2,256,256]{2,1,0:T(8,128)}, f32[2,256,256]{2,1,0:T(8,128)S(1)}, u32[]{:S(2)}) copy-start(f32[2,256,256]{2,1,0:T(8,128)S(1)} %fusion.84) | copy-start | bytes 1572868
  407.4 79.5 %collective-permute-start.4 = (f32[2,256,256]{2,1,0:T(8,128)S(1)}, f32[2,256,256]{2,1,0:T(8,128)S(1)}, u32[]{:S(2)}, u32[]{:S(2)}) collective-permute-start(f32[2,256,256]{2,1,0:T(8,128)S(1)} %fusion.84), channel_id=1, source_target_pairs={{1,0},{2,1},{3,2},{4,3},{5,4},{6,5},{7,6},{8,7},{9,8},{10,9},{11,1... | collective-permute-start | bytes 1572872 | tf_op jit(solution)/shard_map/ppermute | solution.py:17
  486.8 454.0 %all-reduce.10.cloned.1.call-start = ((), (), s32[]{:S(2)}) async-start(), calls=%async_computation.3 | async-start | bytes 1572864 | tf_op jit(solution)/shard_map/psum | solution.py:169
  486.9 1.5 copy-start.23
  487.1 127.8 %collective-permute-start.5 = (f32[2,256,512]{2,1,0:T(8,128)S(1)}, f32[2,256,512]{2,1,0:T(8,128)}, u32[]{:S(2)}, u32[]{:S(2)}) collective-permute-start(f32[2,256,512]{2,1,0:T(8,128)S(1)} %pad_maximum_fusion.4), channel_id=1, source_target_pairs={{16,0},{32,16},{48,32},{64,48},{80,64},{96,80},{112,96},{17,1},{33... | collective-permute-start | bytes 3145736 | tf_op jit(solution)/shard_map/ppermute | solution.py:17
  611.7 3.2 copy-start.24
  613.8 1.0 copy-start.15
  665.6 4.5 copy-start.10
  693.9 4.7 copy-start.8
  698.6 6.9 copy-start.17
  698.6 6.9 copy-start.28
  845.4 8.7 copy-start.25
  845.4 8.7 copy-start.26
  845.4 8.7 copy-start.27
  848.2 92.7 %copy-start.5 = (f32[3,512,512]{2,1,0:T(8,128)S(1)}, f32[3,512,512]{2,1,0:T(8,128)}, u32[]{:S(2)}) copy-start(f32[3,512,512]{2,1,0:T(8,128)} %get-tuple-element.271) | copy-start | bytes 9437188
  848.2 92.7 %collective-permute-start.6 = (f32[3,256,512]{2,1,0:T(8,128)}, f32[3,256,512]{2,1,0:T(8,128)}, u32[]{:S(2)}, u32[]{:S(2)}) collective-permute-start(f32[3,256,512]{2,1,0:T(8,128)} %slice.177), channel_id=1, source_target_pairs={{0,16},{16,32},{32,48},{48,64},{64,80},{80,96},{96,112},{1,17},{17... | collective-permute-start | bytes 4718600 | tf_op jit(solution)/shard_map/ppermute | solution.py:17
  855.1 209.6 %all-reduce.12.cloned.1.call-start = ((), (), s32[]{:S(2)}) async-start(), calls=%async_computation.4 | async-start | bytes 1572864 | tf_op jit(solution)/shard_map/psum | solution.py:169
  942.7 1.2 copy-start.13
  943.8 121.9 %copy-start.16 = (f32[2,256,256]{1,2,0:T(8,128)S(1)}, f32[2,256,256]{1,2,0:T(8,128)}, u32[]{:S(2)}) copy-start(f32[2,256,256]{1,2,0:T(8,128)} %copy-done.15) | copy-start | bytes 1572868
  943.9 123.9 %copy-start.14 = (f32[3,256,512]{2,1,0:T(8,128)S(1)}, f32[3,256,512]{2,1,0:T(8,128)}, u32[]{:S(2)}) copy-start(f32[3,256,512]{2,1,0:T(8,128)} %copy-done.13) | copy-start | bytes 4718596
  943.9 123.9 %collective-permute-start.7 = (f32[3,256,256]{2,1,0:T(8,128)S(1)}, f32[3,256,256]{2,1,0:T(8,128)}, u32[]{:S(2)}, u32[]{:S(2)}) collective-permute-start(f32[3,256,256]{2,1,0:T(8,128)S(1)} %slice.227), channel_id=1, source_target_pairs={{0,1},{1,2},{2,3},{3,4},{4,5},{5,6},{6,7},{7,8},{8,9},{9,10},{10,1... | collective-permute-start | bytes 2359304 | tf_op jit(solution)/shard_map/ppermute | solution.py:17
  1066.8 2.3 copy-start.12
Sparse Core Ops, SparseCore 0:
  397.8 88.9 all-reduce.5
  489.4 122.1 all-reduce.7
  855.2 85.5 all-reduce.9
  943.3 121.3 all-reduce.11
